TPU v7x, 32 devices: a whole 2x2x4 slice. The times are simulated.
32 devices in a mesh: energy: 4 (over y, x), cell: 8 (over z, core).
Axes of the slice: x: 2, y: 2, z: 4, core: 2. Of those that a mesh axis runs over, the one named last changes fastest.
Arguments:
- green_less: float32 [2, 4, 8, 320, 320], P(None, None, 'cell', 'energy'), may hold values from -6 to 6
- green_greater: float32 [2, 4, 8, 320, 320], P(None, None, 'cell', 'energy'), may hold values from -6 to 6
- offsets: int32 [4], replicated, may hold values from 0 to 3, as said below
- orbitals: int32 [8], replicated, may hold values from 192 to 320
- coulomb_diag: float32 [8, 320, 320], P('cell'), may hold values from -0.3125 to 0.3125
- coulomb_up: float32 [8, 320, 320], P('cell'), may hold values from -0.3125 to 0.3125
Outputs:
- screened_diag: float32 [2, 4, 8, 320, 320], P(None, 'energy', 'cell')
- screened_up: float32 [2, 4, 8, 320, 320], P(None, 'energy', 'cell')
Inputs may be any that keep to these rules, and one draw needn't show every extreme that they name: offsets is a permutation of 0 to 3.
All inputs are finite; a program needn't handle non-finite values.
Results may differ from a plain program's by a relative error of at most 0.0003.
Values sent between devices are 32-bit elements; how exact they have to be, the bound alone decides.
A program may use at most 64 MiB of HBM per device.

v0:
```python
import math

import jax
import jax.numpy as jnp
from jax import lax
from jax.sharding import PartitionSpec as P

HIGH = lax.Precision.HIGHEST


def from_behind(block, axis, distance):
    devices = range(lax.axis_size(axis))
    route = [(i - distance, i) for i in devices if i - distance in devices]
    return lax.ppermute(block, axis, route)


def polarize(lesser, greater, offsets):
    count = lesser.shape[1]
    energies = jnp.arange(count, dtype=jnp.int32)

    def single(shift):
        source = energies - shift
        weight = (source >= 0).astype(jnp.float32)
        picked = jnp.take(greater, jnp.clip(source, 0, count - 1), axis=1)
        real_part = lesser[0] * picked[0] + lesser[1] * picked[1]
        imag_part = lesser[1] * picked[0] - lesser[0] * picked[1]
        weight = weight.reshape((count,) + (1,) * (lesser.ndim - 2))
        return jnp.stack([jnp.sum(real_part * weight, axis=0), jnp.sum(imag_part * weight, axis=0)])

    return lax.map(single, offsets) / math.sqrt(count)


def left_mul(coupling, blocks):
    return jnp.einsum("ij,ejk->eik", coupling, blocks, precision=HIGH)


def left_mul_t(coupling, blocks):
    return jnp.einsum("ji,ejk->eik", coupling, blocks, precision=HIGH)


def right_mul(blocks, coupling):
    return jnp.einsum("eij,jk->eik", blocks, coupling, precision=HIGH)


def right_mul_t(blocks, coupling):
    return jnp.einsum("eij,kj->eik", blocks, coupling, precision=HIGH)


def per_device(green_less, green_greater, offsets, orbitals, coulomb_diag, coulomb_up):
    polar = polarize(green_less, green_greater, offsets)
    owned = lax.all_to_all(polar, "energy", split_axis=0, concat_axis=3, tiled=True)
    width = owned.shape[-1]
    en_count = owned.shape[0]
    local = owned.reshape(en_count * 2, width, width)
    cell_index = lax.axis_index("cell")
    cell_count = lax.axis_size("cell")
    rows = jnp.arange(width, dtype=jnp.int32)
    orbit_here = jnp.take(orbitals, cell_index)
    orbit_next = jnp.take(orbitals, jnp.minimum(cell_index + 1, cell_count - 1))
    inside = (rows < orbit_here).astype(jnp.float32)
    inside_next = (rows < orbit_next).astype(jnp.float32)
    vdiag = coulomb_diag[0] * inside[:, None] * inside[None, :]
    vup = coulomb_up[0] * inside[:, None] * inside_next[None, :]
    below = from_behind(jnp.concatenate([local, vup[None]], 0), "cell", 1)
    above = from_behind(jnp.concatenate([local, vdiag[None]], 0), "cell", -1)
    prev_polar = below[:-1]
    prev_up = below[-1]
    next_polar = above[:-1]
    next_diag = above[-1]
    keep = (cell_index < cell_count - 1).astype(jnp.float32)
    a_here = left_mul(vdiag, local)
    a_next = left_mul(vup, next_polar)
    diag = (
        right_mul_t(a_here, vdiag)
        + right_mul_t(a_next, vup)
        + right_mul(left_mul_t(prev_up, prev_polar), prev_up)
    )
    upper = right_mul(a_here, vup) * keep + right_mul_t(a_next, next_diag)
    diag = jnp.moveaxis(diag.reshape(en_count, 2, width, width), 0, 1)[:, :, None]
    upper = jnp.moveaxis(upper.reshape(en_count, 2, width, width), 0, 1)[:, :, None]
    return (diag, upper)


def solution(mesh):
    in_specs = (
        P(None, None, "cell", "energy", None),
        P(None, None, "cell", "energy", None),
        P(),
        P(),
        P("cell", None, None),
        P("cell", None, None),
    )
    out_specs = (P(None, "energy", "cell", None, None), P(None, "energy", "cell", None, None))
    return jax.shard_map(
        per_device, mesh=mesh, in_specs=in_specs, out_specs=out_specs, check_vma=False
    )
```

profile of v0, /device:TPU:1, one launch (start us, length us, event | category | flops | bytes accessed | tf_op | source)
XLA Modules:
  0.0 77.4 jit_solution(14919829609802453852)
XLA Ops:
  0.6 20.9 %while.13 = (s32[]{:T(128)}, f32[4,2,1,80,320]{4,3,2,1,0:T(8,128)S(1)}, f32[2,4,1,80,320]{4,3,2,1,0:T(8,128)}, s32[4]{0:T(128)}, f32[2,4,1,80,320]{4,3,2,1,0:T(8,128)}, /*index=5*/s32[]{:T(128)}) while((s32[]{:T(128)}, f32[4,2,1,80,320]{4,3,2,1,0:T(8,128)S(1)}, f32[2,4,1,80,320]{4,3,2,1,0:T(8,128)}, s32[4]{0:T(128)}, ...), condition=%wide.region_3.4_spmd.clone, body=%wide.region_0.3_spmd.clone.sunk | while | flops 1229886 | bytes 8892625 | solution.py:30
  0.7 1.2 %dynamic_slice.6 = s32[1]{0:T(128)} dynamic-slice(s32[4]{0:T(128)} %get-tuple-element.149, s32[]{:T(128)} %get-tuple-element.140), dynamic_slice_sizes={1} | dynamic-slice | bytes 12 | tf_op jit(solution)/shard_map/while/body/jit(dynamic_index_in_dim)/dynamic_slice | solution.py:30
  2.6 1.8 %gather_fusion = f32[4,2,80,320]{3,2,1,0:T(8,128)S(1)} fusion(f32[2,4,80,320]{3,2,1,0:T(8,128)} %bitcast.149, s32[1024]{0:T(1024)S(1)} %pad_clamp_fusion.2), kind=kCustom, calls=%fused_computation.clone.clone.1 | custom fusion | bytes 1638416 | tf_op jit(solution)/shard_map/while/body/eval_jaxpr/jit(_take)/gather | solution.py:24
  5.9 1.2 %dynamic_slice.6 = s32[1]{0:T(128)} dynamic-slice(s32[4]{0:T(128)} %get-tuple-element.149, s32[]{:T(128)} %get-tuple-element.140), dynamic_slice_sizes={1} | dynamic-slice | bytes 12 | tf_op jit(solution)/shard_map/while/body/jit(dynamic_index_in_dim)/dynamic_slice | solution.py:30
  7.8 1.8 %gather_fusion = f32[4,2,80,320]{3,2,1,0:T(8,128)S(1)} fusion(f32[2,4,80,320]{3,2,1,0:T(8,128)} %bitcast.149, s32[1024]{0:T(1024)S(1)} %pad_clamp_fusion.2), kind=kCustom, calls=%fused_computation.clone.clone.1 | custom fusion | bytes 1638416 | tf_op jit(solution)/shard_map/while/body/eval_jaxpr/jit(_take)/gather | solution.py:24
  11.1 1.2 %dynamic_slice.6 = s32[1]{0:T(128)} dynamic-slice(s32[4]{0:T(128)} %get-tuple-element.149, s32[]{:T(128)} %get-tuple-element.140), dynamic_slice_sizes={1} | dynamic-slice | bytes 12 | tf_op jit(solution)/shard_map/while/body/jit(dynamic_index_in_dim)/dynamic_slice | solution.py:30
  13.0 1.8 %gather_fusion = f32[4,2,80,320]{3,2,1,0:T(8,128)S(1)} fusion(f32[2,4,80,320]{3,2,1,0:T(8,128)} %bitcast.149, s32[1024]{0:T(1024)S(1)} %pad_clamp_fusion.2), kind=kCustom, calls=%fused_computation.clone.clone.1 | custom fusion | bytes 1638416 | tf_op jit(solution)/shard_map/while/body/eval_jaxpr/jit(_take)/gather | solution.py:24
  16.3 1.2 %dynamic_slice.6 = s32[1]{0:T(128)} dynamic-slice(s32[4]{0:T(128)} %get-tuple-element.149, s32[]{:T(128)} %get-tuple-element.140), dynamic_slice_sizes={1} | dynamic-slice | bytes 12 | tf_op jit(solution)/shard_map/while/body/jit(dynamic_index_in_dim)/dynamic_slice | solution.py:30
  18.2 1.8 %gather_fusion = f32[4,2,80,320]{3,2,1,0:T(8,128)S(1)} fusion(f32[2,4,80,320]{3,2,1,0:T(8,128)} %bitcast.149, s32[1024]{0:T(1024)S(1)} %pad_clamp_fusion.2), kind=kCustom, calls=%fused_computation.clone.clone.1 | custom fusion | bytes 1638416 | tf_op jit(solution)/shard_map/while/body/eval_jaxpr/jit(_take)/gather | solution.py:24
  22.5 4.4 %all-to-all-start = ((f32[4,2,1,80,320]{4,3,1,2,0:T(8,128)}), f32[4,2,1,80,320]{4,3,1,2,0:T(8,128)S(1)}, u32[]{:S(2)}, u32[]{:S(2)}) async-start(f32[4,2,1,80,320]{4,3,1,2,0:T(8,128)} %bitcast_multiply_fusion.4), calls=%async_computation | async-start | bytes 1966080 | tf_op jit(solution)/shard_map/all_to_all | solution.py:51
  30.4 8.9 %all-to-all-done = f32[4,2,1,80,320]{4,3,1,2,0:T(8,128)S(1)} async-done(((f32[4,2,1,80,320]{4,3,1,2,0:T(8,128)}), f32[4,2,1,80,320]{4,3,1,2,0:T(8,128)S(1)}, u32[]{:S(2)}, u32[]{:S(2)}) %all-to-all-start) | async-done | bytes 819232 | tf_op jit(solution)/shard_map/all_to_all | solution.py:51
  39.8 1.2 %pad_maximum_fusion = f32[3,320,320]{1,2,0:T(8,128)} fusion(f32[1,320,320]{1,2,0:T(8,128)S(1)} %get-tuple-element.90, f32[2,320,320]{1,2,0:T(8,128)S(1)} %copy.58), kind=kLoop, calls=%fused_computation.22 | loop fusion | flops 307200 | bytes 2457600 | tf_op jit(solution)/shard_map/concatenate | solution.py:65
  41.0 3.4 %collective-permute-start = (f32[3,320,320]{1,2,0:T(8,128)}, f32[3,320,320]{1,2,0:T(8,128)S(1)}, u32[]{:S(2)}, u32[]{:S(2)}) collective-permute-start(f32[3,320,320]{1,2,0:T(8,128)} %pad_maximum_fusion), channel_id=1, source_target_pairs={{1,0},{2,1},{3,2},{4,3},{5,4},{6,5},{7,6},{9,8},{10,9},{11,10},{12... | collective-permute-start | bytes 3686408 | tf_op jit(solution)/shard_map/ppermute | solution.py:14
  44.4 2.0 %copy.61 = f32[1,320,320]{2,1,0:T(8,128)} copy(f32[1,320,320]{1,2,0:T(8,128)} %get-tuple-element.89) | data formatting | bytes 819200 | tf_op jit(solution)/shard_map/mul | solution.py:63
  47.6 3.5 %collective-permute-start.1 = (f32[3,320,320]{2,1,0:T(8,128)S(1)}, f32[3,320,320]{2,1,0:T(8,128)S(1)}, u32[]{:S(2)}, u32[]{:S(2)}) collective-permute-start(f32[3,320,320]{2,1,0:T(8,128)S(1)} %pad_maximum_fusion.1), channel_id=1, source_target_pairs={{0,1},{1,2},{2,3},{3,4},{4,5},{5,6},{6,7},{8,9},{9,10},{10,11},{11... | collective-permute-start | bytes 3686408 | tf_op jit(solution)/shard_map/ppermute | solution.py:14
  51.0 2.2 %convolution_bitcast_fusion.2 = f32[2,320,320]{1,2,0:T(8,128)S(1)} fusion(f32[2,320,320]{2,1,0:T(8,128)S(1)} %bitcast.152, f32[1,320,320]{1,2,0:T(8,128)S(1)} %get-tuple-element.90), kind=kOutput, calls=%fused_computation.32 | convolution fusion | flops 786432000 | bytes 2048000 | tf_op jit(solution)/shard_map/ij,ejk->eik/dot_general | solution.py:34
  53.3 3.7 %fusion.16 = f32[2,320,320]{2,1,0:T(8,128)S(1)} fusion(f32[2,320,320]{1,2,0:T(8,128)S(1)} %convolution_bitcast_fusion.2, f32[1,320,320]{2,1,0:T(8,128)S(1)} %copy-done.3, f32[320]{0:T(512)S(1)} %get-tuple-element.93), kind=kOutput, calls=%fused_computation.42 | convolution fusion | flops 786636800 | bytes 2049280 | tf_op jit(solution)/shard_map/eij,kj->eik/dot_general | solution.py:46
  57.0 2.3 %convolution_multiply_fusion = f32[2,320,320]{2,1,0:T(8,128)S(1)} fusion(f32[2,320,320]{1,2,0:T(8,128)S(1)} %convolution_bitcast_fusion.2, f32[]{:T(128)S(6)} %convert_element_type.30, f32[1,320,320]{2,1,0:T(8,128)S(1)} %copy-done.1, f32[320]{0:T(512)S(1)} %get-tuple-element.94, f32[320]{0:T(512)S(1)} %get-tuple-element.93), kind=kOutput, calls=%fused_computation.26 | convolution fusion | flops 786841600 | bytes 2050564 | tf_op jit(solution)/shard_map/eij,jk->eik/dot_general | solution.py:42
  59.3 3.6 %collective-permute-done = f32[3,320,320]{1,2,0:T(8,128)S(1)} collective-permute-done((f32[3,320,320]{1,2,0:T(8,128)}, f32[3,320,320]{1,2,0:T(8,128)S(1)}, u32[]{:S(2)}, u32[]{:S(2)}) %collective-permute-start) | collective-permute-done | bytes 1228832 | tf_op jit(solution)/shard_map/ppermute | solution.py:14
  62.9 2.1 %convolution_bitcast_fusion.1 = f32[2,320,320]{1,2,0:T(8,128)S(1)} fusion(f32[3,320,320]{1,2,0:T(8,128)S(1)} %collective-permute-done, f32[1,320,320]{2,1,0:T(8,128)S(1)} %copy-done.1, f32[320]{0:T(512)S(1)} %get-tuple-element.94, f32[320]{0:T(512)S(1)} %get-tuple-element.93), kind=kOutput, calls=%fused_computation.31 | convolution fusion | flops 786636800 | bytes 2460160 | tf_op jit(solution)/shard_map/ij,ejk->eik/dot_general | solution.py:34
  64.9 3.4 %fusion.9 = f32[2,1,1,320,320]{4,3,2,1,0:T(8,128)} fusion(f32[2,320,320]{2,1,0:T(8,128)S(1)} %convolution_multiply_fusion, f32[2,320,320]{1,2,0:T(8,128)S(1)} %convolution_bitcast_fusion.1, f32[3,320,320]{1,2,0:T(8,128)S(1)} %collective-permute-done), kind=kOutput, calls=%fused_computation.25 | convolution fusion | flops 786636800 | bytes 3276800 | tf_op jit(solution)/shard_map/eij,kj->eik/dot_general | solution.py:46
  68.3 3.7 %convolution_add_fusion.2 = f32[2,320,320]{2,1,0:T(8,128)S(1)} fusion(f32[2,320,320]{2,1,0:T(8,128)S(1)} %fusion.16, f32[2,320,320]{1,2,0:T(8,128)S(1)} %convolution_bitcast_fusion.1, f32[1,320,320]{2,1,0:T(8,128)S(1)} %copy-done.1, f32[320]{0:T(512)S(1)} %get-tuple-element.94, f32[320]{0:T(512)S(1)} %get-tuple-element.93), kind=kOutput, calls=%fused_computation.29 | convolution fusion | flops 786841600 | bytes 2869760 | tf_op jit(solution)/shard_map/eij,kj->eik/dot_general | solution.py:46
  72.1 2.2 %convolution_bitcast_fusion = f32[2,320,320]{1,2,0:T(8,128)S(1)} fusion(f32[3,320,320]{2,1,0:T(8,128)S(1)} %collective-permute-done.1), kind=kOutput, calls=%fused_computation.30 | convolution fusion | flops 786432000 | bytes 2785280 | tf_op jit(solution)/shard_map/ji,ejk->eik/dot_general | solution.py:38
  74.3 3.2 %fusion.10 = f32[2,1,1,320,320]{4,3,2,1,0:T(8,128)} fusion(f32[2,320,320]{2,1,0:T(8,128)S(1)} %convolution_add_fusion.2, f32[2,320,320]{1,2,0:T(8,128)S(1)} %convolution_bitcast_fusion, f32[3,320,320]{2,1,0:T(8,128)S(1)} %collective-permute-done.1), kind=kOutput, calls=%fused_computation.28 | convolution fusion | flops 786636800 | bytes 3276800 | tf_op jit(solution)/shard_map/eij,jk->eik/dot_general | solution.py:42
  (51 shorter events, 13.2 us)
Async XLA Ops:
  4.4 1.2 %copy-start = (f32[2,4,1,80,320]{4,3,2,1,0:T(8,128)S(1)}, f32[2,4,1,80,320]{4,3,2,1,0:T(8,128)}, u32[]{:S(2)}) copy-start(f32[2,4,1,80,320]{4,3,2,1,0:T(8,128)} %get-tuple-element.148) | copy-start | bytes 2457604 | tf_op jit(solution)/shard_map/while
  9.6 1.2 %copy-start = (f32[2,4,1,80,320]{4,3,2,1,0:T(8,128)S(1)}, f32[2,4,1,80,320]{4,3,2,1,0:T(8,128)}, u32[]{:S(2)}) copy-start(f32[2,4,1,80,320]{4,3,2,1,0:T(8,128)} %get-tuple-element.148) | copy-start | bytes 2457604 | tf_op jit(solution)/shard_map/while
  14.8 1.2 %copy-start = (f32[2,4,1,80,320]{4,3,2,1,0:T(8,128)S(1)}, f32[2,4,1,80,320]{4,3,2,1,0:T(8,128)}, u32[]{:S(2)}) copy-start(f32[2,4,1,80,320]{4,3,2,1,0:T(8,128)} %get-tuple-element.148) | copy-start | bytes 2457604 | tf_op jit(solution)/shard_map/while
  20.0 1.2 %copy-start = (f32[2,4,1,80,320]{4,3,2,1,0:T(8,128)S(1)}, f32[2,4,1,80,320]{4,3,2,1,0:T(8,128)}, u32[]{:S(2)}) copy-start(f32[2,4,1,80,320]{4,3,2,1,0:T(8,128)} %get-tuple-element.148) | copy-start | bytes 2457604 | tf_op jit(solution)/shard_map/while
  22.5 4.4 %copy-start.2 = (f32[1,320,320]{2,1,0:T(8,128)S(1)}, f32[1,320,320]{2,1,0:T(8,128)}, u32[]{:S(2)}) copy-start(f32[1,320,320]{2,1,0:T(8,128)} %param.12) | copy-start | bytes 1228804
  22.5 4.6 %copy-start.1 = (f32[1,320,320]{2,1,0:T(8,128)S(1)}, f32[1,320,320]{2,1,0:T(8,128)}, u32[]{:S(2)}) copy-start(f32[1,320,320]{2,1,0:T(8,128)} %param.13) | copy-start | bytes 1228804
  22.5 16.8 %all-to-all-start = ((f32[4,2,1,80,320]{4,3,1,2,0:T(8,128)}), f32[4,2,1,80,320]{4,3,1,2,0:T(8,128)S(1)}, u32[]{:S(2)}, u32[]{:S(2)}) async-start(f32[4,2,1,80,320]{4,3,1,2,0:T(8,128)} %bitcast_multiply_fusion.4), calls=%async_computation | async-start | bytes 1966080 | tf_op jit(solution)/shard_map/all_to_all | solution.py:51
  26.9 0.7 copy-start.4
  41.0 21.9 %collective-permute-start = (f32[3,320,320]{1,2,0:T(8,128)}, f32[3,320,320]{1,2,0:T(8,128)S(1)}, u32[]{:S(2)}, u32[]{:S(2)}) collective-permute-start(f32[3,320,320]{1,2,0:T(8,128)} %pad_maximum_fusion), channel_id=1, source_target_pairs={{1,0},{2,1},{3,2},{4,3},{5,4},{6,5},{7,6},{9,8},{10,9},{11,10},{12... | collective-permute-start | bytes 3686408 | tf_op jit(solution)/shard_map/ppermute | solution.py:14
  47.5 5.7 %copy-start.3 = (f32[1,320,320]{2,1,0:T(8,128)S(1)}, f32[1,320,320]{2,1,0:T(8,128)}, u32[]{:S(2)}) copy-start(f32[1,320,320]{2,1,0:T(8,128)} %param.12) | copy-start | bytes 1228804
  47.6 24.5 %collective-permute-start.1 = (f32[3,320,320]{2,1,0:T(8,128)S(1)}, f32[3,320,320]{2,1,0:T(8,128)S(1)}, u32[]{:S(2)}, u32[]{:S(2)}) collective-permute-start(f32[3,320,320]{2,1,0:T(8,128)S(1)} %pad_maximum_fusion.1), channel_id=1, source_target_pairs={{0,1},{1,2},{2,3},{3,4},{4,5},{5,6},{6,7},{8,9},{9,10},{10,11},{11... | collective-permute-start | bytes 3686408 | tf_op jit(solution)/shard_map/ppermute | solution.py:14
where the time goes:
time: 78.1 us; the launch traced here: 77.4 us
  matrix products  22.7 us (29%)
  local copies, waits for them, and re-layouts  17.3 us (22%)
  waiting for transfers between devices  12.5 us (16%)
  other arithmetic  11.4 us (15%)
  starting transfers between devices  11.2 us (14%)
  between operations  2.02 us (3%)
    dot_general x3, matrix products, right_mul_t(): return jnp.einsum('eij,kj->eik', blocks, coupling, precision=HIGH)  10.8 us
    all_to_all x1, waiting for transfers between devices, per_device(): lax.all_to_all(polar, 'energy', split_axis=0, concat_axis=3, tiled=True)  8.91 us
    gather x4, local copies, waits for them, and re-layouts, single(): picked = jnp.take(greater, jnp.clip(source, 0, count - 1), axis=1)  7.25 us
    ppermute x2, starting transfers between devices, from_behind(): return lax.ppermute(block, axis, route)  6.85 us
    dot_general x2, matrix products, right_mul(): return jnp.einsum('eij,jk->eik', blocks, coupling, precision=HIGH)  5.43 us
    dynamic_slice x4, local copies, waits for them, and re-layouts, polarize(): return lax.map(single, offsets) / math.sqrt(count)  4.97 us
    all_to_all x1, starting transfers between devices, per_device(): lax.all_to_all(polar, 'energy', split_axis=0, concat_axis=3, tiled=True)  4.4 us
    dot_general x2, matrix products, left_mul(): return jnp.einsum('ij,ejk->eik', coupling, blocks, precision=HIGH)  4.3 us
  transfers between devices with their start and end apart: 3, of which 2 were waited for; matrix products, arithmetic and copies ran while one was open for 29% of the time, Pallas kernels for 0%

commit v1 on v0

v1 whole, which is shorter than its diff:
```python
import functools
import math

import jax
import jax.numpy as jnp
from jax import lax
from jax.experimental import pallas as pl
from jax.experimental.pallas import tpu as pltpu
from jax.sharding import PartitionSpec as P

MESH = pl.DeviceIdType.MESH
F32 = jnp.float32
BF16 = jnp.bfloat16
HERE, NEXT, PREV = 0, 1, 2


def pack(first, second, main):
    return jnp.concatenate(
        [first[:, :main], second[:, :main], first[:, main:], second[:, main:]], axis=1
    )


def unpack(both, main, width):
    edge = 2 * main + width - main
    first = jnp.concatenate([both[:, :main], both[:, 2 * main:edge]], axis=1)
    second = jnp.concatenate([both[:, main:2 * main], both[:, edge:]], axis=1)
    return first, second


def halves(x):
    high = x.astype(BF16).astype(F32)
    return high, x - high


def lane_pad(parts):
    total = sum(p.shape[1] for p in parts)
    extra = -total % 128
    if extra:
        parts = parts + [jnp.zeros((parts[0].shape[0], extra), F32)]
    return jnp.concatenate(parts, axis=1).astype(BF16)


def row_pad(parts):
    total = sum(p.shape[0] for p in parts)
    extra = -total % 128
    if extra:
        parts = parts + [jnp.zeros((extra, parts[0].shape[1]), F32)]
    return jnp.concatenate(parts, axis=0).astype(BF16)


def left_operand(block):
    high, low = halves(block)
    return lane_pad([high, low, high])


def left_rows(rows):
    high, low = halves(rows)
    return row_pad([high, high, low])


def right_operand(main, tail):
    high, low = halves(main)
    end_high, end_low = halves(tail)
    return jnp.concatenate(
        [high.astype(BF16), low.astype(BF16), high.astype(BF16), lane_pad([end_high, end_low, end_high])],
        axis=1,
    )


def right_rows(block, main):
    high, low = halves(block)
    return row_pad(
        [high[:main], high[:main], low[:main], high[main:], high[main:], low[main:]]
    )


def dot(a, b):
    return jnp.dot(a, b, preferred_element_type=F32)


def kernel(
    energies, cells, offsets, orbitals, less_hbm, greater_hbm, vdiag_hbm, vup_hbm,
    diag_hbm, upper_hbm,
    less, greater, vdiag, vup, shifted, outgoing, polar, beside, v_out, v_in,
    left, right, right_prev, a_sum, o_sum, diag, upper,
    in_sem, out_sem, swap_send, swap_recv, side_send, side_recv, v_send, v_recv,
):
    me = lax.axis_index("energy")
    cell = lax.axis_index("cell")
    rows, width = less.shape[2], less.shape[3]
    main = width // 128 * 128
    half = width // 2
    has_next = cell < cells - 1
    has_prev = cell > 0

    def peer(k):
        if energies & (energies - 1):
            return lax.rem(me + k, energies)
        other, bit = me, 1
        while bit <= k:
            if k & bit:
                other = other + bit * (1 - 2 * lax.rem(me // bit, 2))
            bit *= 2
        return other

    loads = [
        pltpu.make_async_copy(src, dst, in_sem.at[i])
        for i, (src, dst) in enumerate(
            [(vdiag_hbm, vdiag), (vup_hbm, vup), (less_hbm, less), (greater_hbm, greater)]
        )
    ]
    for load in loads:
        load.start()

    barrier = pltpu.get_barrier_semaphore()
    for k in range(1, energies):
        pl.semaphore_signal(barrier, inc=1, device_id=(peer(k), cell), device_id_type=MESH)

    @pl.when(has_next)
    def _():
        pl.semaphore_signal(barrier, inc=1, device_id=(me, cell + 1), device_id_type=MESH)

    @pl.when(has_prev)
    def _():
        pl.semaphore_signal(barrier, inc=1, device_id=(me, cell - 1), device_id_type=MESH)

    @pl.when(jnp.logical_not(has_prev))
    def _():
        beside[0] = jnp.zeros(beside.shape[1:], F32)
        v_in[0] = jnp.zeros(v_in.shape[1:], F32)

    @pl.when(jnp.logical_not(has_next))
    def _():
        beside[1] = jnp.zeros(beside.shape[1:], F32)
        v_in[1] = jnp.zeros(v_in.shape[1:], F32)

    def v_copy(side):
        return pltpu.make_async_remote_copy(
            src_ref=v_out.at[side], dst_ref=v_in.at[side],
            send_sem=v_send.at[side], recv_sem=v_recv.at[side],
            device_id=(me, cell + 1 - 2 * side), device_id_type=MESH,
        )

    def side_copy(side, slot):
        return pltpu.make_async_remote_copy(
            src_ref=polar.at[slot], dst_ref=beside.at[side, slot],
            send_sem=side_send.at[side, slot], recv_sem=side_recv.at[side, slot],
            device_id=(me, cell + 1 - 2 * side), device_id_type=MESH,
        )

    def swap_copy(k):
        return pltpu.make_async_remote_copy(
            src_ref=outgoing.at[peer(k)], dst_ref=polar.at[me],
            send_sem=swap_send.at[k], recv_sem=swap_recv.at[k],
            device_id=(peer(k), cell), device_id_type=MESH,
        )

    def swap_arrival(k):
        back = k if not energies & (energies - 1) else energies - k
        return pltpu.make_async_remote_copy(
            src_ref=outgoing.at[peer(back)], dst_ref=polar.at[peer(back)],
            send_sem=swap_send.at[k], recv_sem=swap_recv.at[k],
            device_id=(peer(back), cell), device_id_type=MESH,
        ), peer(back)

    def forward(slot):
        @pl.when(has_next)
        def _():
            side_copy(0, slot).start()

        @pl.when(has_prev)
        def _():
            side_copy(1, slot).start()

    here_orbitals = orbitals[cell]
    next_orbitals = jnp.where(has_next, orbitals[jnp.minimum(cell + 1, cells - 1)], 0)
    row = lax.broadcasted_iota(jnp.int32, (width, width), 0)
    col = lax.broadcasted_iota(jnp.int32, (width, width), 1)
    loads[0].wait()
    loads[1].wait()
    vd = jnp.where((row < here_orbitals) & (col < here_orbitals), vdiag[...], 0.0)
    vu = jnp.where((row < here_orbitals) & (col < next_orbitals), vup[...], 0.0)
    vdiag[...] = vd
    vup[...] = vu
    v_out[0] = pack(vu[:half], vu[half:], main)
    v_out[1] = pack(vd[:half], vd[half:], main)

    met = energies - 1 + jnp.where(has_next, 1, 0) + jnp.where(has_prev, 1, 0)
    pl.semaphore_wait(barrier, met)

    @pl.when(has_next)
    def _():
        v_copy(0).start()

    @pl.when(has_prev)
    def _():
        v_copy(1).start()

    loads[2].wait()
    loads[3].wait()
    scale = 1.0 / math.sqrt(energies)

    def polarize(step, carry):
        at = pl.ds(pl.multiple_of(step * 8, 8), 8)
        l_re = [less[0, m, at, :] for m in range(energies)]
        l_im = [less[1, m, at, :] for m in range(energies)]
        g_re = [greater[0, m, at, :] for m in range(energies)]
        g_im = [greater[1, m, at, :] for m in range(energies)]
        for shift in range(energies):
            real = imag = None
            for m in range(shift, energies):
                r = l_re[m] * g_re[m - shift] + l_im[m] * g_im[m - shift]
                i = l_im[m] * g_re[m - shift] - l_re[m] * g_im[m - shift]
                real = r if real is None else real + r
                imag = i if imag is None else imag + i
            shifted[shift, at, :] = pack(real * scale, imag * scale, main)
        return carry

    lax.fori_loop(0, rows // 8, polarize, 0)
    for k in reversed(range(1, energies)):
        n = peer(k)
        outgoing[n] = shifted[offsets[n]]
        swap_copy(k).start()
    polar[me] = shifted[offsets[me]]
    forward(me)

    def cut(which, block):
        for e in range(energies):
            left[which, e] = left_operand(block[:, e * rows:(e + 1) * rows])

    vd = vdiag[...]
    cut(HERE, vd)
    right[HERE] = right_rows(pack(vd.T, vup[...], main), main)
    vu = vup[...]
    cut(NEXT, vu)

    def add_left(which, slot, block, first):
        product = dot(left[which, slot], left_rows(block))
        if first:
            a_sum[which] = product
        else:
            a_sum[which] += product

    def split(which):
        a = a_sum[which]
        edge = 2 * main + width - main
        return (
            right_operand(a[:, :main], a[:, 2 * main:edge]),
            right_operand(a[:, main:2 * main], a[:, edge:]),
        )

    def arrive(k):
        copy, slot = swap_arrival(k)
        copy.wait_recv()
        forward(slot)
        return slot

    slots = [me]

    def take_here(k):
        if k:
            slots.append(arrive(k))
        add_left(HERE, slots[k], polar[slots[k]], k == 0)

    def take_sides(k):
        slot = slots[k]

        @pl.when(has_prev)
        def _():
            side_copy(0, slot).wait_recv()

        @pl.when(has_next)
        def _():
            side_copy(1, slot).wait_recv()

        add_left(PREV, slot, beside[0, slot], k == 0)
        add_left(NEXT, slot, beside[1, slot], k == 0)

    take_here(0)
    early = max(1, energies - 1)
    for k in range(1, early):
        take_here(k)

    @pl.when(has_prev)
    def _():
        v_copy(0).wait_recv()

    @pl.when(has_next)
    def _():
        v_copy(1).wait_recv()

    def whole(packed):
        top, bottom = unpack(packed, main, width)
        return jnp.concatenate([top, bottom], axis=0)

    vp = whole(v_in[0])
    cut(PREV, vp.T)
    right_prev[...] = right_rows(
        jnp.concatenate([vp, jnp.zeros((width, -width % 128), F32)], axis=1), main
    )
    vn = whole(v_in[1])
    right[NEXT] = right_rows(pack(vup[...].T, vn.T, main), main)

    for k in range(early - 1):
        take_sides(k)
    for k in range(early, energies):
        take_here(k)
    for part, operand in enumerate(split(HERE)):
        o_sum[part] = dot(operand, right[HERE])
    for k in range(early - 1, energies):
        take_sides(k)
    for part, (after, before) in enumerate(zip(split(NEXT), split(PREV))):
        total = o_sum[part] + dot(after, right[NEXT])
        from_prev = dot(before, right_prev[...])
        first, second = unpack(total, main, width)
        diag[part] = first + from_prev[:, :width]
        upper[part] = second
        pltpu.make_async_copy(diag.at[part], diag_hbm.at[part], out_sem.at[0, part]).start()
        pltpu.make_async_copy(upper.at[part], upper_hbm.at[part], out_sem.at[1, part]).start()

    for k in range(1, energies):
        swap_copy(k).wait_send()

    @pl.when(has_next)
    def _():
        v_copy(0).wait_send()
        for slot in range(energies):
            side_copy(0, slot).wait_send()

    @pl.when(has_prev)
    def _():
        v_copy(1).wait_send()
        for slot in range(energies):
            side_copy(1, slot).wait_send()

    for part in range(2):
        pltpu.make_async_copy(diag.at[part], diag_hbm.at[part], out_sem.at[0, part]).wait()
        pltpu.make_async_copy(upper.at[part], upper_hbm.at[part], out_sem.at[1, part]).wait()


def solution(mesh):
    energies, cells = mesh.shape["energy"], mesh.shape["cell"]

    def per_device(green_less, green_greater, offsets, orbitals, coulomb_diag, coulomb_up):
        less = jnp.squeeze(green_less, 2)
        greater = jnp.squeeze(green_greater, 2)
        rows, width = less.shape[2], less.shape[3]
        main = width // 128 * 128
        depth = 3 * rows + -3 * rows % 128
        long = 3 * width + -3 * width % 128
        shape = jax.ShapeDtypeStruct((2, width, width), F32)
        anywhere = pl.BlockSpec(memory_space=pl.ANY)
        scalars = pl.BlockSpec(memory_space=pltpu.SMEM)
        dma = pltpu.SemaphoreType.DMA
        products = width * width * width * 2 * 8 * 3
        diag, upper = pl.pallas_call(
            functools.partial(kernel, energies, cells),
            out_shape=(shape, shape),
            in_specs=[scalars, scalars, anywhere, anywhere, anywhere, anywhere],
            out_specs=(anywhere, anywhere),
            scratch_shapes=[
                pltpu.VMEM(less.shape, F32),
                pltpu.VMEM(less.shape, F32),
                pltpu.VMEM((width, width), F32),
                pltpu.VMEM((width, width), F32),
                pltpu.VMEM((energies, rows, 2 * width), F32),
                pltpu.VMEM((energies, rows, 2 * width), F32),
                pltpu.VMEM((energies, rows, 2 * width), F32),
                pltpu.VMEM((2, energies, rows, 2 * width), F32),
                pltpu.VMEM((2, width // 2, 2 * width), F32),
                pltpu.VMEM((2, width // 2, 2 * width), F32),
                pltpu.VMEM((3, energies, width, depth), BF16),
                pltpu.VMEM((2, long, 2 * width), BF16),
                pltpu.VMEM((long, width + -width % 128), BF16),
                pltpu.VMEM((3, width, 2 * width), F32),
                pltpu.VMEM((2, width, 2 * width), F32),
                pltpu.VMEM((2, width, width), F32),
                pltpu.VMEM((2, width, width), F32),
                dma((4,)),
                dma((2, 2)),
                dma((energies,)),
                dma((energies,)),
                dma((2, energies)),
                dma((2, energies)),
                dma((2,)),
                dma((2,)),
            ],
            compiler_params=pltpu.CompilerParams(
                collective_id=0, has_side_effects=True, vmem_limit_bytes=48 * 1024 * 1024
            ),
            cost_estimate=pl.CostEstimate(
                flops=2 * products, bytes_accessed=4 * less.size * 4, transcendentals=0
            ),
            name="screen",
        )(offsets, orbitals, less, greater, coulomb_diag[0], coulomb_up[0])
        return diag[:, None, None], upper[:, None, None]

    in_specs = (
        P(None, None, "cell", "energy", None),
        P(None, None, "cell", "energy", None),
        P(),
        P(),
        P("cell", None, None),
        P("cell", None, None),
    )
    out_specs = (P(None, "energy", "cell", None, None), P(None, "energy", "cell", None, None))
    return jax.shard_map(
        per_device, mesh=mesh, in_specs=in_specs, out_specs=out_specs, check_vma=False
    )
```

time: 78.1 us -> 38.4 us (0.49)
  Pallas kernels: 0 us -> 30.4 us
  matrix products: 22.7 us -> 0 us
  waiting for transfers between devices: 12.5 us -> 0 us
  other arithmetic: 11.4 us -> 0 us
  starting transfers between devices: 11.2 us -> 0 us
  local copies, waits for them, and re-layouts: 17.3 us -> 7.01 us
  between operations: 2.02 us -> 0.66 us
    pallas_call x0 -> x1, Pallas kernels: none -> 30.4 us  [per_device(): pl.pallas_call(functools.partial(kernel, energies, cells), out_shape=(sha...]
    dot_general x8 -> x0, matrix products: 22.7 us -> none  [the longest x3 10.8 us: right_mul_t(): return jnp.einsum('eij,kj->eik', blocks, coupling, precision=HIGH)]
    all_to_all x1 -> x0, waiting for transfers between devices: 8.91 us -> none  [per_device(): lax.all_to_all(polar, 'energy', split_axis=0, concat_axis=3, tiled=True)]
    gather x4 -> x0, local copies, waits for them, and re-layouts: 7.25 us -> none  [single(): picked = jnp.take(greater, jnp.clip(source, 0, count - 1), axis=1)]
    ppermute x2 -> x0, starting transfers between devices: 6.85 us -> none  [from_behind(): return lax.ppermute(block, axis, route)]
    unnamed x10 -> x14, local copies, waits for them, and re-layouts: 0.66 us -> 7.01 us
    dynamic_slice x4 -> x0, local copies, waits for them, and re-layouts: 4.97 us -> none  [polarize(): return lax.map(single, offsets) / math.sqrt(count)]
    all_to_all x1 -> x0, starting transfers between devices: 4.4 us -> none  [per_device(): lax.all_to_all(polar, 'energy', split_axis=0, concat_axis=3, tiled=True)]
  transfers between devices with their start and end apart: 3 -> 0, of which waited for: 2 -> 0; matrix products, arithmetic and copies ran while one was open for 29% -> 0% of each run, Pallas kernels for 0% -> 0%
where the time goes in v1:
time: 38.4 us; the launch traced here: 38.1 us
  Pallas kernels  30.4 us (79%)
  local copies, waits for them, and re-layouts  7.01 us (18%)
  between operations  0.66 us (2%)
    pallas_call x1, Pallas kernels, per_device(): pl.pallas_call(functools.partial(kernel, energies, cells), out_shape=(sha...  30.4 us
    unnamed x14, local copies, waits for them, and re-layouts  7.01 us

profile of v1, /device:TPU:1, one launch (start us, length us, event | category | flops | bytes accessed | tf_op | source)
XLA Modules:
  0.0 38.1 jit_solution(14425469285261148069)
XLA Ops:
  0.6 0.0 copy-start.4
  0.6 0.0 copy-start.5
  0.7 0.6 %copy-done.4 = s32[4]{0:T(128)S(1)} copy-done((s32[4]{0:T(128)S(1)}, s32[4]{0:T(128)}, u32[]{:S(2)}) %copy-start.4) | copy-done | bytes 40
  1.3 0.0 copy-done.5
  1.3 0.0 copy-start
  1.3 1.2 %copy-done = f32[2,4,1,80,320]{4,3,2,1,0:T(8,128)S(1)} copy-done((f32[2,4,1,80,320]{4,3,2,1,0:T(8,128)S(1)}, f32[2,4,1,80,320]{4,3,2,1,0:T(8,128)}, u32[]{:S(2)}) %copy-start) | copy-done | bytes 819224
  2.5 0.0 copy-start.1
  2.5 1.2 %copy-done.1 = f32[2,4,1,80,320]{4,3,2,1,0:T(8,128)S(1)} copy-done((f32[2,4,1,80,320]{4,3,2,1,0:T(8,128)S(1)}, f32[2,4,1,80,320]{4,3,2,1,0:T(8,128)}, u32[]{:S(2)}) %copy-start.1) | copy-done | bytes 819224
  3.7 0.0 copy-start.2
  3.7 1.0 %copy-done.2 = f32[1,320,320]{2,1,0:T(8,128)S(1)} copy-done((f32[1,320,320]{2,1,0:T(8,128)S(1)}, f32[1,320,320]{2,1,0:T(8,128)}, u32[]{:S(2)}) %copy-start.2) | copy-done | bytes 409624
  4.7 0.0 copy-start.3
  4.7 1.0 %copy-done.3 = f32[1,320,320]{2,1,0:T(8,128)S(1)} copy-done((f32[1,320,320]{2,1,0:T(8,128)S(1)}, f32[1,320,320]{2,1,0:T(8,128)}, u32[]{:S(2)}) %copy-start.3) | copy-done | bytes 409624
  5.8 30.4 %screen.1 = (f32[2,320,320]{2,1,0:T(8,128)S(1)}, f32[2,320,320]{2,1,0:T(8,128)S(1)}) custom-call(s32[4]{0:T(128)S(1)} %copy-done.4, s32[8]{0:T(128)S(1)} %copy-done.5, f32[2,4,80,320]{3,2,1,0:T(8,128)S(1)} %bitcast.12, f32[2,4,80,320]{3,2,1,0:T(8,128)S(1)} %bitcast.13, f32[320,320]{1,0:T(8,128)S(1)} %bitcast.14, f32[320,320]{1,0:T(8,128)S(1)} %bitcast.15), custom_call_target="tpu_custom_call" | custom-call | flops 3145728000 | bytes 3276800 | tf_op jit(solution)/shard_map/screen/pallas_call | solution.py:356
  36.2 0.9 %copy.12 = f32[2,1,1,320,320]{4,3,2,1,0:T(8,128)} copy(f32[2,1,1,320,320]{4,3,2,1,0:T(8,128)S(1)} %bitcast.11) | data formatting | bytes 1638400
  37.2 0.9 %copy.13 = f32[2,1,1,320,320]{4,3,2,1,0:T(8,128)} copy(f32[2,1,1,320,320]{4,3,2,1,0:T(8,128)S(1)} %bitcast.10) | data formatting | bytes 1638400
Async XLA Ops:
  0.6 0.7 %copy-start.4 = (s32[4]{0:T(128)S(1)}, s32[4]{0:T(128)}, u32[]{:S(2)}) copy-start(s32[4]{0:T(128)} %offsets.1) | copy-start | bytes 52
  0.6 0.7 %copy-start.5 = (s32[8]{0:T(128)S(1)}, s32[8]{0:T(128)}, u32[]{:S(2)}) copy-start(s32[8]{0:T(128)} %orbitals.1) | copy-start | bytes 100
  1.3 1.2 %copy-start = (f32[2,4,1,80,320]{4,3,2,1,0:T(8,128)S(1)}, f32[2,4,1,80,320]{4,3,2,1,0:T(8,128)}, u32[]{:S(2)}) copy-start(f32[2,4,1,80,320]{4,3,2,1,0:T(8,128)} %param.6) | copy-start | bytes 2457604
  2.5 1.2 %copy-start.1 = (f32[2,4,1,80,320]{4,3,2,1,0:T(8,128)S(1)}, f32[2,4,1,80,320]{4,3,2,1,0:T(8,128)}, u32[]{:S(2)}) copy-start(f32[2,4,1,80,320]{4,3,2,1,0:T(8,128)} %param.7) | copy-start | bytes 2457604
  3.7 1.0 %copy-start.2 = (f32[1,320,320]{2,1,0:T(8,128)S(1)}, f32[1,320,320]{2,1,0:T(8,128)}, u32[]{:S(2)}) copy-start(f32[1,320,320]{2,1,0:T(8,128)} %param.10) | copy-start | bytes 1228804
  4.7 1.0 %copy-start.3 = (f32[1,320,320]{2,1,0:T(8,128)S(1)}, f32[1,320,320]{2,1,0:T(8,128)}, u32[]{:S(2)}) copy-start(f32[1,320,320]{2,1,0:T(8,128)} %param.11) | copy-start | bytes 1228804

commit v2 on v1

--- a/solution.py
+++ b/solution.py
@@ -80,10 +80,10 @@
 
 def kernel(
     energies, cells, offsets, orbitals, less_hbm, greater_hbm, vdiag_hbm, vup_hbm,
-    diag_hbm, upper_hbm,
+    diag, upper,
     less, greater, vdiag, vup, shifted, outgoing, polar, beside, v_out, v_in,
-    left, right, right_prev, a_sum, o_sum, diag, upper,
-    in_sem, out_sem, swap_send, swap_recv, side_send, side_recv, v_send, v_recv,
+    left, right, a_sum, o_sum,
+    in_sem, swap_send, swap_recv, side_send, side_recv, v_send, v_recv, trade_send,
 ):
     me = lax.axis_index("energy")
     cell = lax.axis_index("cell")
@@ -134,12 +134,45 @@
         beside[1] = jnp.zeros(beside.shape[1:], F32)
         v_in[1] = jnp.zeros(v_in.shape[1:], F32)
 
-    def v_copy(side):
+    odd = lax.rem(cell, 2)
+    trading = energies % 4 == 0
+    trader = peer(1) * (1 - odd) + peer(2) * odd
+
+    def half_of(side):
+        return lax.rem(me, 2) if side == 0 else lax.rem(me // 2, 2)
+
+    def v_copy(side, part):
         return pltpu.make_async_remote_copy(
-            src_ref=v_out.at[side], dst_ref=v_in.at[side],
-            send_sem=v_send.at[side], recv_sem=v_recv.at[side],
+            src_ref=v_out.at[side, part], dst_ref=v_in.at[side, part],
+            send_sem=v_send.at[side, part], recv_sem=v_recv.at[side, part],
             device_id=(me, cell + 1 - 2 * side), device_id_type=MESH,
         )
+
+    def trade_copy(side, part):
+        return pltpu.make_async_remote_copy(
+            src_ref=v_in.at[side, part], dst_ref=v_in.at[side, part],
+            send_sem=trade_send, recv_sem=v_recv.at[side, part],
+            device_id=(trader, cell), device_id_type=MESH,
+        )
+
+    def each_v(act):
+        for side, there in ((0, has_next), (1, has_prev)):
+            if not trading:
+                @pl.when(there)
+                def _():
+                    act(v_copy(side, 0))
+                    act(v_copy(side, 1))
+                continue
+            crosses = odd == 1 - side
+
+            @pl.when(there & crosses)
+            def _():
+                act(v_copy(side, half_of(side)))
+
+            @pl.when(there & jnp.logical_not(crosses))
+            def _():
+                act(v_copy(side, 0))
+                act(v_copy(side, 1))
 
     def side_copy(side, slot):
         return pltpu.make_async_remote_copy(
@@ -182,19 +215,15 @@
     vu = jnp.where((row < here_orbitals) & (col < next_orbitals), vup[...], 0.0)
     vdiag[...] = vd
     vup[...] = vu
-    v_out[0] = pack(vu[:half], vu[half:], main)
-    v_out[1] = pack(vd[:half], vd[half:], main)
+    for part in range(2):
+        a, b, c = part * half // 2, (part + 1) * half // 2, half
+        v_out[0, part] = pack(vu[a:b], vu[c + a:c + b], main)
+        v_out[1, part] = pack(vd[a:b], vd[c + a:c + b], main)
 
     met = energies - 1 + jnp.where(has_next, 1, 0) + jnp.where(has_prev, 1, 0)
     pl.semaphore_wait(barrier, met)
 
-    @pl.when(has_next)
-    def _():
-        v_copy(0).start()
-
-    @pl.when(has_prev)
-    def _():
-        v_copy(1).start()
+    each_v(lambda copy: copy.start())
 
     loads[2].wait()
     loads[3].wait()
@@ -217,7 +246,7 @@
         return carry
 
     lax.fori_loop(0, rows // 8, polarize, 0)
-    for k in reversed(range(1, energies)):
+    for k in range(1, energies):
         n = peer(k)
         outgoing[n] = shifted[offsets[n]]
         swap_copy(k).start()
@@ -230,9 +259,13 @@
 
     vd = vdiag[...]
     cut(HERE, vd)
-    right[HERE] = right_rows(pack(vd.T, vup[...], main), main)
-    vu = vup[...]
-    cut(NEXT, vu)
+    if trading:
+        for side, there in ((0, has_prev), (1, has_next)):
+            @pl.when(there & (odd == side))
+            def _():
+                part = half_of(side)
+                v_copy(side, part).wait_recv()
+                trade_copy(side, part).start()
 
     def add_left(which, slot, block, first):
         product = dot(left[which, slot], left_rows(block))
@@ -262,80 +295,83 @@
             slots.append(arrive(k))
         add_left(HERE, slots[k], polar[slots[k]], k == 0)
 
-    def take_sides(k):
+    def take_side(side, k):
         slot = slots[k]
 
-        @pl.when(has_prev)
+        @pl.when(jnp.where(side == 0, has_prev, has_next))
         def _():
-            side_copy(0, slot).wait_recv()
-
-        @pl.when(has_next)
-        def _():
-            side_copy(1, slot).wait_recv()
-
-        add_left(PREV, slot, beside[0, slot], k == 0)
-        add_left(NEXT, slot, beside[1, slot], k == 0)
+            side_copy(side, slot).wait_recv()
+
+        add_left(2 - side, slot, beside[side, slot], k == 0)
+
+    def take_right(which, first):
+        for part, operand in enumerate(split(which)):
+            product = dot(operand, right[which])
+            if first:
+                o_sum[part] = product
+            else:
+                o_sum[part] += product
 
     take_here(0)
-    early = max(1, energies - 1)
-    for k in range(1, early):
+    right[HERE] = right_rows(pack(vd.T, vup[...], main), main)
+    vu = vup[...]
+    cut(NEXT, vu)
+    late, early = odd, 1 - odd
+    last = energies - 1
+    for k in range(1, last):
         take_here(k)
 
-    @pl.when(has_prev)
-    def _():
-        v_copy(0).wait_recv()
-
-    @pl.when(has_next)
-    def _():
-        v_copy(1).wait_recv()
-
-    def whole(packed):
-        top, bottom = unpack(packed, main, width)
-        return jnp.concatenate([top, bottom], axis=0)
-
-    vp = whole(v_in[0])
+    for side, there in ((0, has_prev), (1, has_next)):
+        for part in range(2):
+            mine = (odd == side) & (half_of(side) == part) if trading else False
+
+            @pl.when(there & jnp.logical_not(mine))
+            def _():
+                v_copy(side, part).wait_recv()
+
+    def whole(side):
+        parts = [unpack(v_in[side, part], main, width) for part in range(2)]
+        return jnp.concatenate([p[0] for p in parts] + [p[1] for p in parts], axis=0)
+
+    vp = whole(0)
     cut(PREV, vp.T)
-    right_prev[...] = right_rows(
-        jnp.concatenate([vp, jnp.zeros((width, -width % 128), F32)], axis=1), main
-    )
-    vn = whole(v_in[1])
+    right[PREV] = right_rows(pack(vp, jnp.zeros_like(vp), main), main)
+    vn = whole(1)
     right[NEXT] = right_rows(pack(vup[...].T, vn.T, main), main)
 
-    for k in range(early - 1):
-        take_sides(k)
-    for k in range(early, energies):
-        take_here(k)
-    for part, operand in enumerate(split(HERE)):
-        o_sum[part] = dot(operand, right[HERE])
-    for k in range(early - 1, energies):
-        take_sides(k)
-    for part, (after, before) in enumerate(zip(split(NEXT), split(PREV))):
-        total = o_sum[part] + dot(after, right[NEXT])
-        from_prev = dot(before, right_prev[...])
-        first, second = unpack(total, main, width)
-        diag[part] = first + from_prev[:, :width]
-        upper[part] = second
-        pltpu.make_async_copy(diag.at[part], diag_hbm.at[part], out_sem.at[0, part]).start()
-        pltpu.make_async_copy(upper.at[part], upper_hbm.at[part], out_sem.at[1, part]).start()
+    for k in range(last):
+        take_side(early, k)
+        if k < last - 1:
+            take_side(late, k)
+    take_here(last)
+    take_right(HERE, True)
+    if last:
+        take_side(late, last - 1)
+    take_side(early, last)
+    take_right(2 - early, False)
+    take_side(late, last)
+    for part, operand in enumerate(split(2 - late)):
+        total = o_sum[part] + dot(operand, right[2 - late])
+        diag[part], upper[part] = unpack(total, main, width)
 
     for k in range(1, energies):
         swap_copy(k).wait_send()
+    each_v(lambda copy: copy.wait_send())
+    if trading:
+        for side, there in ((0, has_prev), (1, has_next)):
+            @pl.when(there & (odd == side))
+            def _():
+                trade_copy(side, half_of(side)).wait_send()
 
     @pl.when(has_next)
     def _():
-        v_copy(0).wait_send()
         for slot in range(energies):
             side_copy(0, slot).wait_send()
 
     @pl.when(has_prev)
     def _():
-        v_copy(1).wait_send()
         for slot in range(energies):
             side_copy(1, slot).wait_send()
-
-    for part in range(2):
-        pltpu.make_async_copy(diag.at[part], diag_hbm.at[part], out_sem.at[0, part]).wait()
-        pltpu.make_async_copy(upper.at[part], upper_hbm.at[part], out_sem.at[1, part]).wait()
 
 
 def solution(mesh):
@@ -349,7 +385,7 @@
         depth = 3 * rows + -3 * rows % 128
         long = 3 * width + -3 * width % 128
         shape = jax.ShapeDtypeStruct((2, width, width), F32)
-        anywhere = pl.BlockSpec(memory_space=pl.ANY)
+        anywhere = pl.BlockSpec(memory_space=pltpu.HBM)
         scalars = pl.BlockSpec(memory_space=pltpu.SMEM)
         dma = pltpu.SemaphoreType.DMA
         products = width * width * width * 2 * 8 * 3
@@ -357,7 +393,7 @@
             functools.partial(kernel, energies, cells),
             out_shape=(shape, shape),
             in_specs=[scalars, scalars, anywhere, anywhere, anywhere, anywhere],
-            out_specs=(anywhere, anywhere),
+            out_specs=(pl.BlockSpec(memory_space=pltpu.VMEM),) * 2,
             scratch_shapes=[
                 pltpu.VMEM(less.shape, F32),
                 pltpu.VMEM(less.shape, F32),
@@ -367,26 +403,23 @@
                 pltpu.VMEM((energies, rows, 2 * width), F32),
                 pltpu.VMEM((energies, rows, 2 * width), F32),
                 pltpu.VMEM((2, energies, rows, 2 * width), F32),
-                pltpu.VMEM((2, width // 2, 2 * width), F32),
-                pltpu.VMEM((2, width // 2, 2 * width), F32),
+                pltpu.VMEM((2, 2, width // 4, 2 * width), F32),
+                pltpu.VMEM((2, 2, width // 4, 2 * width), F32),
                 pltpu.VMEM((3, energies, width, depth), BF16),
-                pltpu.VMEM((2, long, 2 * width), BF16),
-                pltpu.VMEM((long, width + -width % 128), BF16),
+                pltpu.VMEM((3, long, 2 * width), BF16),
                 pltpu.VMEM((3, width, 2 * width), F32),
                 pltpu.VMEM((2, width, 2 * width), F32),
-                pltpu.VMEM((2, width, width), F32),
-                pltpu.VMEM((2, width, width), F32),
                 dma((4,)),
-                dma((2, 2)),
                 dma((energies,)),
                 dma((energies,)),
                 dma((2, energies)),
                 dma((2, energies)),
-                dma((2,)),
-                dma((2,)),
+                dma((2, 2)),
+                dma((2, 2)),
+                dma,
             ],
             compiler_params=pltpu.CompilerParams(
-                collective_id=0, has_side_effects=True, vmem_limit_bytes=48 * 1024 * 1024
+                collective_id=0, has_side_effects=True, vmem_limit_bytes=62914560
             ),
             cost_estimate=pl.CostEstimate(
                 flops=2 * products, bytes_accessed=4 * less.size * 4, transcendentals=0

time: 38.4 us -> 32.7 us (0.85)
  local copies, waits for them, and re-layouts: 7.01 us -> 3.24 us
  Pallas kernels: 30.4 us -> 28.6 us
    unnamed x14 -> x4, local copies, waits for them, and re-layouts: 7.01 us -> 3.24 us
    pallas_call x1, Pallas kernels: 30.4 us -> 28.6 us  [per_device(): pl.pallas_call(functools.partial(kernel, energies, cells), out_shape=(sha...]
where the time goes in v2:
time: 32.7 us; the launch traced here: 32.5 us
  Pallas kernels  28.6 us (87%)
  local copies, waits for them, and re-layouts  3.24 us (10%)
  between operations  0.65 us (2%)
    pallas_call x1, Pallas kernels, per_device(): pl.pallas_call(functools.partial(kernel, energies, cells), out_shape=(sha...  28.6 us
    unnamed x4, local copies, waits for them, and re-layouts  3.24 us

profile of v2, /device:TPU:1, one launch (start us, length us, event | category | flops | bytes accessed | tf_op | source)
XLA Modules:
  0.0 32.5 jit_solution(14178718226684522585)
XLA Ops:
  0.6 28.6 %screen.1 = (f32[2,320,320]{2,1,0:T(8,128)}, f32[2,320,320]{2,1,0:T(8,128)}) custom-call(s32[4]{0:T(128)} %offsets.1, s32[8]{0:T(128)} %orbitals.1, f32[2,4,80,320]{3,2,1,0:T(8,128)} %bitcast.12, f32[2,4,80,320]{3,2,1,0:T(8,128)} %bitcast.13, f32[320,320]{1,0:T(8,128)} %bitcast.14, f32[320,320]{1,0:T(8,128)} %bitcast.15), custom_call_target="tpu_custom_call" | custom-call | flops 3145728000 | bytes 3276800 | tf_op jit(solution)/shard_map/screen/pallas_call | solution.py:392
  29.3 0.0 copy-start
  29.3 2.3 %copy.12 = f32[2,1,1,320,320]{4,3,2,1,0:T(8,128)} copy(f32[2,1,1,320,320]{4,3,2,1,0:T(8,128)} %bitcast.11) | data formatting | bytes 1638400
  31.6 0.0 copy-done
  31.6 0.9 %copy.13 = f32[2,1,1,320,320]{4,3,2,1,0:T(8,128)} copy(f32[2,1,1,320,320]{4,3,2,1,0:T(8,128)S(1)} %bitcast.10) | data formatting | bytes 1638400
Async XLA Ops:
  29.3 2.3 %copy-start = (f32[2,320,320]{2,1,0:T(8,128)S(1)}, f32[2,320,320]{2,1,0:T(8,128)}, u32[]{:S(2)}) copy-start(f32[2,320,320]{2,1,0:T(8,128)} %get-tuple-element.5) | copy-start | bytes 2457604

commit v3 on v1

--- a/solution.py
+++ b/solution.py
@@ -80,9 +80,9 @@
 
 def kernel(
     energies, cells, offsets, orbitals, less_hbm, greater_hbm, vdiag_hbm, vup_hbm,
-    diag_hbm, upper_hbm,
+    diag_out, upper_out,
     less, greater, vdiag, vup, shifted, outgoing, polar, beside, v_out, v_in,
-    left, right, right_prev, a_sum, o_sum, diag, upper,
+    left, right, a_sum, o_sum, diag, upper,
     in_sem, out_sem, swap_send, swap_recv, side_send, side_recv, v_send, v_recv,
 ):
     me = lax.axis_index("energy")
@@ -134,6 +134,10 @@
         beside[1] = jnp.zeros(beside.shape[1:], F32)
         v_in[1] = jnp.zeros(v_in.shape[1:], F32)
 
+    late = lax.rem(cell, 2)
+    early = 1 - late
+    last = energies - 1
+
     def v_copy(side):
         return pltpu.make_async_remote_copy(
             src_ref=v_out.at[side], dst_ref=v_in.at[side],
@@ -141,36 +145,57 @@
             device_id=(me, cell + 1 - 2 * side), device_id_type=MESH,
         )
 
-    def side_copy(side, slot):
+    cut_at = rows // 2 // 8 * 8
+
+    def pieces(k):
+        if k and k == last and cut_at:
+            return [(0, pl.ds(0, cut_at)), (1, pl.ds(cut_at, rows - cut_at))]
+        return [(0, pl.ds(0, rows))]
+
+    def side_copy(side, k, piece, at):
+        slot = slots[k]
         return pltpu.make_async_remote_copy(
-            src_ref=polar.at[slot], dst_ref=beside.at[side, slot],
-            send_sem=side_send.at[side, slot], recv_sem=side_recv.at[side, slot],
+            src_ref=polar.at[slot, at], dst_ref=beside.at[side, slot, at],
+            send_sem=side_send.at[side, k, piece], recv_sem=side_recv.at[side, k, piece],
             device_id=(me, cell + 1 - 2 * side), device_id_type=MESH,
         )
 
-    def swap_copy(k):
-        return pltpu.make_async_remote_copy(
-            src_ref=outgoing.at[peer(k)], dst_ref=polar.at[me],
-            send_sem=swap_send.at[k], recv_sem=swap_recv.at[k],
-            device_id=(peer(k), cell), device_id_type=MESH,
-        )
-
-    def swap_arrival(k):
-        back = k if not energies & (energies - 1) else energies - k
-        return pltpu.make_async_remote_copy(
-            src_ref=outgoing.at[peer(back)], dst_ref=polar.at[peer(back)],
-            send_sem=swap_send.at[k], recv_sem=swap_recv.at[k],
-            device_id=(peer(back), cell), device_id_type=MESH,
-        ), peer(back)
-
-    def forward(slot):
+    def side_copies(side, k):
+        return [side_copy(side, k, piece, at) for piece, at in pieces(k)]
+
+    def swap_copies(k):
+        return [
+            pltpu.make_async_remote_copy(
+                src_ref=outgoing.at[peer(k), at], dst_ref=polar.at[me, at],
+                send_sem=swap_send.at[k, piece], recv_sem=swap_recv.at[k, piece],
+                device_id=(peer(k), cell), device_id_type=MESH,
+            )
+            for piece, at in pieces(k)
+        ]
+
+    def source(k):
+        return peer(k if not energies & (energies - 1) else energies - k)
+
+    slots = [me] + [source(k) for k in range(1, energies)]
+
+    def swap_arrivals(k):
+        return [
+            pltpu.make_async_remote_copy(
+                src_ref=outgoing.at[slots[k], at], dst_ref=polar.at[slots[k], at],
+                send_sem=swap_send.at[k, piece], recv_sem=swap_recv.at[k, piece],
+                device_id=(slots[k], cell), device_id_type=MESH,
+            )
+            for piece, at in pieces(k)
+        ]
+
+    def forward(k, piece, at):
         @pl.when(has_next)
         def _():
-            side_copy(0, slot).start()
+            side_copy(0, k, piece, at).start()
 
         @pl.when(has_prev)
         def _():
-            side_copy(1, slot).start()
+            side_copy(1, k, piece, at).start()
 
     here_orbitals = orbitals[cell]
     next_orbitals = jnp.where(has_next, orbitals[jnp.minimum(cell + 1, cells - 1)], 0)
@@ -217,12 +242,14 @@
         return carry
 
     lax.fori_loop(0, rows // 8, polarize, 0)
-    for k in reversed(range(1, energies)):
+    polar[me] = shifted[offsets[me]]
+    forward(0, *pieces(0)[0])
+    for k in range(1, energies):
         n = peer(k)
         outgoing[n] = shifted[offsets[n]]
-        swap_copy(k).start()
-    polar[me] = shifted[offsets[me]]
-    forward(me)
+        if k < last or last == 1:
+            for copy in swap_copies(k):
+                copy.start()
 
     def cut(which, block):
         for e in range(energies):
@@ -231,8 +258,7 @@
     vd = vdiag[...]
     cut(HERE, vd)
     right[HERE] = right_rows(pack(vd.T, vup[...], main), main)
-    vu = vup[...]
-    cut(NEXT, vu)
+    cut(NEXT, vup[...])
 
     def add_left(which, slot, block, first):
         product = dot(left[which, slot], left_rows(block))
@@ -250,35 +276,39 @@
         )
 
     def arrive(k):
-        copy, slot = swap_arrival(k)
-        copy.wait_recv()
-        forward(slot)
-        return slot
-
-    slots = [me]
+        for copy, (piece, at) in zip(swap_arrivals(k), pieces(k)):
+            copy.wait_recv()
+            forward(k, piece, at)
 
     def take_here(k):
-        if k:
-            slots.append(arrive(k))
         add_left(HERE, slots[k], polar[slots[k]], k == 0)
 
-    def take_sides(k):
-        slot = slots[k]
-
-        @pl.when(has_prev)
+    def take_side(side, k):
+        @pl.when(jnp.where(side == 0, has_prev, has_next))
         def _():
-            side_copy(0, slot).wait_recv()
-
-        @pl.when(has_next)
-        def _():
-            side_copy(1, slot).wait_recv()
-
-        add_left(PREV, slot, beside[0, slot], k == 0)
-        add_left(NEXT, slot, beside[1, slot], k == 0)
+            for copy in side_copies(side, k):
+                copy.wait_recv()
+
+        add_left(2 - side, slots[k], beside[side, slots[k]], k == 0)
+
+    def take_right(which, first):
+        for part, operand in enumerate(split(which)):
+            product = dot(operand, right[which])
+            if first:
+                o_sum[part] = product
+            else:
+                o_sum[part] += product
 
     take_here(0)
-    early = max(1, energies - 1)
-    for k in range(1, early):
+    for k in range(1, last):
+        arrive(k)
+    if last > 1:
+        for k in range(1, last):
+            for copy in swap_copies(k):
+                copy.wait_send()
+        for copy in swap_copies(last):
+            copy.start()
+    for k in range(1, last):
         take_here(k)
 
     @pl.when(has_prev)
@@ -289,53 +319,70 @@
     def _():
         v_copy(1).wait_recv()
 
-    def whole(packed):
-        top, bottom = unpack(packed, main, width)
+    def whole(side):
+        top, bottom = unpack(v_in[side], main, width)
         return jnp.concatenate([top, bottom], axis=0)
 
-    vp = whole(v_in[0])
+    vp = whole(0)
     cut(PREV, vp.T)
-    right_prev[...] = right_rows(
-        jnp.concatenate([vp, jnp.zeros((width, -width % 128), F32)], axis=1), main
-    )
-    vn = whole(v_in[1])
+    right[PREV] = right_rows(pack(vp, jnp.zeros_like(vp), main), main)
+    vn = whole(1)
     right[NEXT] = right_rows(pack(vup[...].T, vn.T, main), main)
 
-    for k in range(early - 1):
-        take_sides(k)
-    for k in range(early, energies):
-        take_here(k)
-    for part, operand in enumerate(split(HERE)):
-        o_sum[part] = dot(operand, right[HERE])
-    for k in range(early - 1, energies):
-        take_sides(k)
-    for part, (after, before) in enumerate(zip(split(NEXT), split(PREV))):
-        total = o_sum[part] + dot(after, right[NEXT])
-        from_prev = dot(before, right_prev[...])
-        first, second = unpack(total, main, width)
-        diag[part] = first + from_prev[:, :width]
-        upper[part] = second
-        pltpu.make_async_copy(diag.at[part], diag_hbm.at[part], out_sem.at[0, part]).start()
-        pltpu.make_async_copy(upper.at[part], upper_hbm.at[part], out_sem.at[1, part]).start()
-
-    for k in range(1, energies):
-        swap_copy(k).wait_send()
+    for k in range(last):
+        take_side(early, k)
+        if k < last - 1:
+            take_side(late, k)
+    if last:
+        arrive(last)
+        take_here(last)
+    take_right(HERE, True)
+    if last:
+        take_side(late, last - 1)
+    take_side(early, last)
+    take_right(2 - early, False)
+    take_side(late, last)
+    writes = []
+    for part, operand in enumerate(split(2 - late)):
+        total = o_sum[part] + dot(operand, right[2 - late])
+        diag[part], upper[part] = unpack(total, main, width)
+        for i, (src, dst) in enumerate([(diag, diag_out), (upper, upper_out)]):
+            writes.append(pltpu.make_async_copy(src.at[part], dst.at[part], out_sem.at[i, part]))
+            writes[-1].start()
+
+    for copy in swap_copies(last) if last else []:
+        copy.wait_send()
 
     @pl.when(has_next)
     def _():
         v_copy(0).wait_send()
-        for slot in range(energies):
-            side_copy(0, slot).wait_send()
+        for k in range(energies):
+            for copy in side_copies(0, k):
+                copy.wait_send()
 
     @pl.when(has_prev)
     def _():
         v_copy(1).wait_send()
-        for slot in range(energies):
-            side_copy(1, slot).wait_send()
-
-    for part in range(2):
-        pltpu.make_async_copy(diag.at[part], diag_hbm.at[part], out_sem.at[0, part]).wait()
-        pltpu.make_async_copy(upper.at[part], upper_hbm.at[part], out_sem.at[1, part]).wait()
+        for k in range(energies):
+            for copy in side_copies(1, k):
+                copy.wait_send()
+
+    for write in writes:
+        write.wait()
+
+
+def deliver(diag_in, upper_in, diag, upper, sem):
+    rows = diag_in.shape[1]
+    middle = rows // 16 * 8
+    copies = []
+    for i, (src, dst) in enumerate([(diag_in, diag), (upper_in, upper)]):
+        for part in range(2):
+            for j, at in enumerate([pl.ds(0, middle), pl.ds(middle, rows - middle)]):
+                copies.append(pltpu.make_async_copy(src.at[part, at], dst.at[part, at], sem.at[i, part, j]))
+    for copy in copies:
+        copy.start()
+    for copy in copies:
+        copy.wait()
 
 
 def solution(mesh):
@@ -349,7 +396,7 @@
         depth = 3 * rows + -3 * rows % 128
         long = 3 * width + -3 * width % 128
         shape = jax.ShapeDtypeStruct((2, width, width), F32)
-        anywhere = pl.BlockSpec(memory_space=pl.ANY)
+        anywhere = pl.BlockSpec(memory_space=pltpu.HBM)
         scalars = pl.BlockSpec(memory_space=pltpu.SMEM)
         dma = pltpu.SemaphoreType.DMA
         products = width * width * width * 2 * 8 * 3
@@ -370,29 +417,40 @@
                 pltpu.VMEM((2, width // 2, 2 * width), F32),
                 pltpu.VMEM((2, width // 2, 2 * width), F32),
                 pltpu.VMEM((3, energies, width, depth), BF16),
-                pltpu.VMEM((2, long, 2 * width), BF16),
-                pltpu.VMEM((long, width + -width % 128), BF16),
+                pltpu.VMEM((3, long, 2 * width), BF16),
                 pltpu.VMEM((3, width, 2 * width), F32),
                 pltpu.VMEM((2, width, 2 * width), F32),
                 pltpu.VMEM((2, width, width), F32),
                 pltpu.VMEM((2, width, width), F32),
                 dma((4,)),
                 dma((2, 2)),
-                dma((energies,)),
-                dma((energies,)),
-                dma((2, energies)),
-                dma((2, energies)),
+                dma((energies, 2)),
+                dma((energies, 2)),
+                dma((2, energies, 2)),
+                dma((2, energies, 2)),
                 dma((2,)),
                 dma((2,)),
             ],
             compiler_params=pltpu.CompilerParams(
-                collective_id=0, has_side_effects=True, vmem_limit_bytes=48 * 1024 * 1024
+                collective_id=0, has_side_effects=True, vmem_limit_bytes=62914560
             ),
             cost_estimate=pl.CostEstimate(
                 flops=2 * products, bytes_accessed=4 * less.size * 4, transcendentals=0
             ),
             name="screen",
         )(offsets, orbitals, less, greater, coulomb_diag[0], coulomb_up[0])
+        diag, upper = pl.pallas_call(
+            deliver,
+            out_shape=(shape, shape),
+            in_specs=[pl.BlockSpec(memory_space=pl.ANY)] * 2,
+            out_specs=(pl.BlockSpec(memory_space=pl.ANY),) * 2,
+            scratch_shapes=[dma((2, 2, 2))],
+            cost_estimate=pl.CostEstimate(
+                flops=0, bytes_accessed=16 * width * width * 2, transcendentals=0
+            ),
+            compiler_params=pltpu.CompilerParams(vmem_limit_bytes=60 * 1024 * 1024),
+            name="deliver",
+        )(diag, upper)
         return diag[:, None, None], upper[:, None, None]
 
     in_specs = (

time: 38.4 us -> 85.6 us (2.23)
  Pallas kernels: 30.4 us -> 84.8 us
  local copies, waits for them, and re-layouts: 7.01 us -> 0 us
    pallas_call x0 -> x1, Pallas kernels: none -> 60.7 us  [per_device(): pl.pallas_call(deliver, out_shape=(shape, shape), in_specs=[pl.BlockSpec(...]
    unnamed x14 -> x0, local copies, waits for them, and re-layouts: 7.01 us -> none
    pallas_call x1, Pallas kernels: 30.4 us -> 24.1 us  [per_device(): pl.pallas_call(functools.partial(kernel, energies, cells), out_shape=(sha...]
where the time goes in v3:
time: 85.6 us; the launch traced here: 85.5 us
  Pallas kernels  84.8 us (99%)
    pallas_call x1, Pallas kernels, per_device(): pl.pallas_call(deliver, out_shape=(shape, shape), in_specs=[pl.BlockSpec(...  60.7 us
    pallas_call x1, Pallas kernels, per_device(): pl.pallas_call(functools.partial(kernel, energies, cells), out_shape=(sha...  24.1 us

profile of v3, /device:TPU:1, one launch (start us, length us, event | category | flops | bytes accessed | tf_op | source)
XLA Modules:
  0.0 85.5 jit_solution(4881306733693841590)
XLA Ops:
  0.6 24.1 %screen.1 = (f32[2,320,320]{2,1,0:T(8,128)}, f32[2,320,320]{2,1,0:T(8,128)}) custom-call(s32[4]{0:T(128)} %offsets.1, s32[8]{0:T(128)} %orbitals.1, f32[2,4,80,320]{3,2,1,0:T(8,128)} %bitcast.10, f32[2,4,80,320]{3,2,1,0:T(8,128)} %bitcast.11, f32[320,320]{1,0:T(8,128)} %bitcast.14, f32[320,320]{1,0:T(8,128)} %bitcast.15), custom_call_target="tpu_custom_call" | custom-call | flops 3145728000 | bytes 3276800 | tf_op jit(solution)/shard_map/screen/pallas_call | solution.py:403
  24.7 60.7 %deliver.1 = (f32[2,320,320]{2,1,0:T(8,128)}, f32[2,320,320]{2,1,0:T(8,128)}) custom-call(f32[2,320,320]{2,1,0:T(8,128)} %get-tuple-element.6.diag_in, f32[2,320,320]{2,1,0:T(8,128)} %get-tuple-element.7.upper_in), custom_call_target="tpu_custom_call" | custom-call | bytes 3276800 | tf_op jit(solution)/shard_map/deliver/pallas_call | solution.py:442

commit v4 on v3

--- a/solution.py
+++ b/solution.py
@@ -12,6 +12,8 @@
 F32 = jnp.float32
 BF16 = jnp.bfloat16
 HERE, NEXT, PREV = 0, 1, 2
+SCREEN_BYTES = 60 * 1024 * 1024
+DELIVER_BYTES = 60 * 1024 * 1024
 
 
 def pack(first, second, main):
@@ -82,7 +84,7 @@
     energies, cells, offsets, orbitals, less_hbm, greater_hbm, vdiag_hbm, vup_hbm,
     diag_out, upper_out,
     less, greater, vdiag, vup, shifted, outgoing, polar, beside, v_out, v_in,
-    left, right, a_sum, o_sum, diag, upper,
+    left, right, stack, o_sum, diag, upper,
     in_sem, out_sem, swap_send, swap_recv, side_send, side_recv, v_send, v_recv,
 ):
     me = lax.axis_index("energy")
@@ -103,14 +105,16 @@
             bit *= 2
         return other
 
-    loads = [
-        pltpu.make_async_copy(src, dst, in_sem.at[i])
-        for i, (src, dst) in enumerate(
-            [(vdiag_hbm, vdiag), (vup_hbm, vup), (less_hbm, less), (greater_hbm, greater)]
-        )
-    ]
-    for load in loads:
-        load.start()
+    def load(number, src, dst):
+        pieces_of = []
+        middle = src.shape[0] // 2
+        for i, at in enumerate([pl.ds(0, middle), pl.ds(middle, src.shape[0] - middle)]):
+            pieces_of.append(pltpu.make_async_copy(src.at[at], dst.at[at], in_sem.at[number, i]))
+            pieces_of[-1].start()
+        return pieces_of
+
+    v_loads = load(0, vdiag_hbm, vdiag) + load(1, vup_hbm, vup)
+    loads = load(2, less_hbm, less) + load(3, greater_hbm, greater)
 
     barrier = pltpu.get_barrier_semaphore()
     for k in range(1, energies):
@@ -201,8 +205,8 @@
     next_orbitals = jnp.where(has_next, orbitals[jnp.minimum(cell + 1, cells - 1)], 0)
     row = lax.broadcasted_iota(jnp.int32, (width, width), 0)
     col = lax.broadcasted_iota(jnp.int32, (width, width), 1)
-    loads[0].wait()
-    loads[1].wait()
+    for copy in v_loads:
+        copy.wait()
     vd = jnp.where((row < here_orbitals) & (col < here_orbitals), vdiag[...], 0.0)
     vu = jnp.where((row < here_orbitals) & (col < next_orbitals), vup[...], 0.0)
     vdiag[...] = vd
@@ -221,8 +225,8 @@
     def _():
         v_copy(1).start()
 
-    loads[2].wait()
-    loads[3].wait()
+    for copy in loads:
+        copy.wait()
     scale = 1.0 / math.sqrt(energies)
 
     def polarize(step, carry):
@@ -260,46 +264,34 @@
     right[HERE] = right_rows(pack(vd.T, vup[...], main), main)
     cut(NEXT, vup[...])
 
-    def add_left(which, slot, block, first):
-        product = dot(left[which, slot], left_rows(block))
-        if first:
-            a_sum[which] = product
-        else:
-            a_sum[which] += product
-
-    def split(which):
-        a = a_sum[which]
+    def stacked(block):
         edge = 2 * main + width - main
-        return (
-            right_operand(a[:, :main], a[:, 2 * main:edge]),
-            right_operand(a[:, main:2 * main], a[:, edge:]),
+        return right_operand(
+            jnp.concatenate([block[:, :main], block[:, main:2 * main]], axis=0),
+            jnp.concatenate([block[:, 2 * main:edge], block[:, edge:]], axis=0),
         )
+
+    def add_left(which, block_of):
+        operand = jnp.concatenate([left[which, slots[k]] for k in range(last)], axis=1)
+        facing = jnp.concatenate([left_rows(block_of(slots[k])) for k in range(last)], axis=0)
+        stack[which] = stacked(dot(operand, facing))
 
     def arrive(k):
         for copy, (piece, at) in zip(swap_arrivals(k), pieces(k)):
             copy.wait_recv()
             forward(k, piece, at)
 
-    def take_here(k):
-        add_left(HERE, slots[k], polar[slots[k]], k == 0)
-
-    def take_side(side, k):
+    def wait_side(side, k):
         @pl.when(jnp.where(side == 0, has_prev, has_next))
         def _():
             for copy in side_copies(side, k):
                 copy.wait_recv()
 
-        add_left(2 - side, slots[k], beside[side, slots[k]], k == 0)
-
-    def take_right(which, first):
-        for part, operand in enumerate(split(which)):
-            product = dot(operand, right[which])
-            if first:
-                o_sum[part] = product
-            else:
-                o_sum[part] += product
-
-    take_here(0)
+    def take_side(side):
+        for k in range(last):
+            wait_side(side, k)
+        add_left(2 - side, lambda slot: beside[side, slot])
+
     for k in range(1, last):
         arrive(k)
     if last > 1:
@@ -308,8 +300,7 @@
                 copy.wait_send()
         for copy in swap_copies(last):
             copy.start()
-    for k in range(1, last):
-        take_here(k)
+    add_left(HERE, lambda slot: polar[slot])
 
     @pl.when(has_prev)
     def _():
@@ -329,28 +320,31 @@
     vn = whole(1)
     right[NEXT] = right_rows(pack(vup[...].T, vn.T, main), main)
 
-    for k in range(last):
-        take_side(early, k)
-        if k < last - 1:
-            take_side(late, k)
-    if last:
-        arrive(last)
-        take_here(last)
-    take_right(HERE, True)
-    if last:
-        take_side(late, last - 1)
-    take_side(early, last)
-    take_right(2 - early, False)
-    take_side(late, last)
+    take_side(early)
+    arrive(last)
+    take_side(late)
+    kinds = (HERE, NEXT, PREV)
+    o_sum[...] = dot(
+        jnp.concatenate([stack[which] for which in kinds], axis=1),
+        jnp.concatenate([right[which] for which in kinds], axis=0),
+    )
+    wait_side(early, last)
+    wait_side(late, last)
+
+    slot = slots[last]
+    ends = [polar[slot], beside[1, slot], beside[0, slot]]
+    turned = [dot(stacked(end), right[which]) for which, end in zip(kinds, ends)]
+    operand = jnp.concatenate([left[which, slot] for which in kinds], axis=1)
     writes = []
-    for part, operand in enumerate(split(2 - late)):
-        total = o_sum[part] + dot(operand, right[2 - late])
+    for part in range(2):
+        facing = [left_rows(t[part * rows:(part + 1) * rows]) for t in turned]
+        total = o_sum[part * width:(part + 1) * width, :] + dot(operand, jnp.concatenate(facing, axis=0))
         diag[part], upper[part] = unpack(total, main, width)
         for i, (src, dst) in enumerate([(diag, diag_out), (upper, upper_out)]):
             writes.append(pltpu.make_async_copy(src.at[part], dst.at[part], out_sem.at[i, part]))
             writes[-1].start()
 
-    for copy in swap_copies(last) if last else []:
+    for copy in swap_copies(last):
         copy.wait_send()
 
     @pl.when(has_next)
@@ -371,18 +365,25 @@
         write.wait()
 
 
-def deliver(diag_in, upper_in, diag, upper, sem):
+def deliver(diag_in, upper_in, diag, upper, held, in_sem, out_sem):
     rows = diag_in.shape[1]
     middle = rows // 16 * 8
     copies = []
     for i, (src, dst) in enumerate([(diag_in, diag), (upper_in, upper)]):
         for part in range(2):
             for j, at in enumerate([pl.ds(0, middle), pl.ds(middle, rows - middle)]):
-                copies.append(pltpu.make_async_copy(src.at[part, at], dst.at[part, at], sem.at[i, part, j]))
-    for copy in copies:
-        copy.start()
-    for copy in copies:
-        copy.wait()
+                here = held.at[i, part, at]
+                copies.append((
+                    pltpu.make_async_copy(src.at[part, at], here, in_sem.at[i, part, j]),
+                    pltpu.make_async_copy(here, dst.at[part, at], out_sem.at[i, part, j]),
+                ))
+    for arriving, _ in copies:
+        arriving.start()
+    for arriving, leaving in copies:
+        arriving.wait()
+        leaving.start()
+    for _, leaving in copies:
+        leaving.wait()
 
 
 def solution(mesh):
@@ -418,11 +419,11 @@
                 pltpu.VMEM((2, width // 2, 2 * width), F32),
                 pltpu.VMEM((3, energies, width, depth), BF16),
                 pltpu.VMEM((3, long, 2 * width), BF16),
-                pltpu.VMEM((3, width, 2 * width), F32),
-                pltpu.VMEM((2, width, 2 * width), F32),
+                pltpu.VMEM((3, 2 * width, long), BF16),
+                pltpu.VMEM((2 * width, 2 * width), F32),
                 pltpu.VMEM((2, width, width), F32),
                 pltpu.VMEM((2, width, width), F32),
-                dma((4,)),
+                dma((4, 2)),
                 dma((2, 2)),
                 dma((energies, 2)),
                 dma((energies, 2)),
@@ -432,7 +433,7 @@
                 dma((2,)),
             ],
             compiler_params=pltpu.CompilerParams(
-                collective_id=0, has_side_effects=True, vmem_limit_bytes=62914560
+                collective_id=0, has_side_effects=True, vmem_limit_bytes=SCREEN_BYTES
             ),
             cost_estimate=pl.CostEstimate(
                 flops=2 * products, bytes_accessed=4 * less.size * 4, transcendentals=0
@@ -444,11 +445,11 @@
             out_shape=(shape, shape),
             in_specs=[pl.BlockSpec(memory_space=pl.ANY)] * 2,
             out_specs=(pl.BlockSpec(memory_space=pl.ANY),) * 2,
-            scratch_shapes=[dma((2, 2, 2))],
+            scratch_shapes=[pltpu.VMEM((2,) + shape.shape, F32), dma((2, 2, 2)), dma((2, 2, 2))],
             cost_estimate=pl.CostEstimate(
                 flops=0, bytes_accessed=16 * width * width * 2, transcendentals=0
             ),
-            compiler_params=pltpu.CompilerParams(vmem_limit_bytes=60 * 1024 * 1024),
+            compiler_params=pltpu.CompilerParams(vmem_limit_bytes=DELIVER_BYTES),
             name="deliver",
         )(diag, upper)
         return diag[:, None, None], upper[:, None, None]

time: 85.6 us -> 29.7 us (0.35)
  Pallas kernels: 84.8 us -> 28.9 us
    pallas_call x1, Pallas kernels: 60.7 us -> 2.47 us  [per_device(): pl.pallas_call(deliver, out_shape=(shape, shape), in_specs=[pl.BlockSpec(...]
    pallas_call x1, Pallas kernels: 24.1 us -> 26.4 us  [per_device(): pl.pallas_call(functools.partial(kernel, energies, cells), out_shape=(sha...]
where the time goes in v4:
time: 29.7 us; the launch traced here: 29.5 us
  Pallas kernels  28.9 us (97%)
  between operations  0.64 us (2%)
    pallas_call x1, Pallas kernels, per_device(): pl.pallas_call(functools.partial(kernel, energies, cells), out_shape=(sha...  26.4 us
    pallas_call x1, Pallas kernels, per_device(): pl.pallas_call(deliver, out_shape=(shape, shape), in_specs=[pl.BlockSpec(...  2.47 us

profile of v4, /device:TPU:1, one launch (start us, length us, event | category | flops | bytes accessed | tf_op | source)
XLA Modules:
  0.0 29.5 jit_solution(2374693886234833381)
XLA Ops:
  0.6 26.4 %screen.1 = (f32[2,320,320]{2,1,0:T(8,128)}, f32[2,320,320]{2,1,0:T(8,128)}) custom-call(s32[4]{0:T(128)} %offsets.1, s32[8]{0:T(128)} %orbitals.1, f32[2,4,80,320]{3,2,1,0:T(8,128)} %bitcast.10, f32[2,4,80,320]{3,2,1,0:T(8,128)} %bitcast.11, f32[320,320]{1,0:T(8,128)} %bitcast.14, f32[320,320]{1,0:T(8,128)} %bitcast.15), custom_call_target="tpu_custom_call" | custom-call | flops 3145728000 | bytes 3276800 | tf_op jit(solution)/shard_map/screen/pallas_call | solution.py:404
  27.1 2.5 %deliver.1 = (f32[2,320,320]{2,1,0:T(8,128)}, f32[2,320,320]{2,1,0:T(8,128)}) custom-call(f32[2,320,320]{2,1,0:T(8,128)} %get-tuple-element.6.diag_in, f32[2,320,320]{2,1,0:T(8,128)} %get-tuple-element.7.upper_in), custom_call_target="tpu_custom_call" | custom-call | bytes 3276800 | tf_op jit(solution)/shard_map/deliver/pallas_call | solution.py:443

commit v5 on v4

--- a/solution.py
+++ b/solution.py
@@ -84,7 +84,7 @@
     energies, cells, offsets, orbitals, less_hbm, greater_hbm, vdiag_hbm, vup_hbm,
     diag_out, upper_out,
     less, greater, vdiag, vup, shifted, outgoing, polar, beside, v_out, v_in,
-    left, right, stack, o_sum, diag, upper,
+    left, right, a_sum, o_sum, diag, upper,
     in_sem, out_sem, swap_send, swap_recv, side_send, side_recv, v_send, v_recv,
 ):
     me = lax.axis_index("energy")
@@ -271,15 +271,20 @@
             jnp.concatenate([block[:, 2 * main:edge], block[:, edge:]], axis=0),
         )
 
-    def add_left(which, block_of):
-        operand = jnp.concatenate([left[which, slots[k]] for k in range(last)], axis=1)
-        facing = jnp.concatenate([left_rows(block_of(slots[k])) for k in range(last)], axis=0)
-        stack[which] = stacked(dot(operand, facing))
+    def add_left(which, slot, block, first):
+        product = dot(left[which, slot], left_rows(block))
+        if first:
+            a_sum[which] = product
+        else:
+            a_sum[which] += product
 
     def arrive(k):
         for copy, (piece, at) in zip(swap_arrivals(k), pieces(k)):
             copy.wait_recv()
             forward(k, piece, at)
+
+    def take_here(k):
+        add_left(HERE, slots[k], polar[slots[k]], k == 0)
 
     def wait_side(side, k):
         @pl.when(jnp.where(side == 0, has_prev, has_next))
@@ -287,11 +292,18 @@
             for copy in side_copies(side, k):
                 copy.wait_recv()
 
-    def take_side(side):
-        for k in range(last):
-            wait_side(side, k)
-        add_left(2 - side, lambda slot: beside[side, slot])
-
+    def take_side(side, k):
+        wait_side(side, k)
+        add_left(2 - side, slots[k], beside[side, slots[k]], k == 0)
+
+    def take_right(which, first):
+        product = dot(stacked(a_sum[which]), right[which])
+        if first:
+            o_sum[...] = product
+        else:
+            o_sum[...] += product
+
+    take_here(0)
     for k in range(1, last):
         arrive(k)
     if last > 1:
@@ -300,7 +312,8 @@
                 copy.wait_send()
         for copy in swap_copies(last):
             copy.start()
-    add_left(HERE, lambda slot: polar[slot])
+    for k in range(1, last):
+        take_here(k)
 
     @pl.when(has_prev)
     def _():
@@ -320,25 +333,25 @@
     vn = whole(1)
     right[NEXT] = right_rows(pack(vup[...].T, vn.T, main), main)
 
-    take_side(early)
+    for k in range(last):
+        take_side(early, k)
+        if k < last - 1:
+            take_side(late, k)
     arrive(last)
-    take_side(late)
-    kinds = (HERE, NEXT, PREV)
-    o_sum[...] = dot(
-        jnp.concatenate([stack[which] for which in kinds], axis=1),
-        jnp.concatenate([right[which] for which in kinds], axis=0),
-    )
-    wait_side(early, last)
+    take_here(last)
+    take_right(HERE, True)
+    take_side(late, last - 1)
+    take_side(early, last)
+    take_right(2 - early, False)
+    take_right(2 - late, False)
+
     wait_side(late, last)
-
     slot = slots[last]
-    ends = [polar[slot], beside[1, slot], beside[0, slot]]
-    turned = [dot(stacked(end), right[which]) for which, end in zip(kinds, ends)]
-    operand = jnp.concatenate([left[which, slot] for which in kinds], axis=1)
+    turned = dot(stacked(beside[late, slot]), right[2 - late])
     writes = []
     for part in range(2):
-        facing = [left_rows(t[part * rows:(part + 1) * rows]) for t in turned]
-        total = o_sum[part * width:(part + 1) * width, :] + dot(operand, jnp.concatenate(facing, axis=0))
+        facing = left_rows(turned[part * rows:(part + 1) * rows])
+        total = o_sum[part * width:(part + 1) * width, :] + dot(left[2 - late, slot], facing)
         diag[part], upper[part] = unpack(total, main, width)
         for i, (src, dst) in enumerate([(diag, diag_out), (upper, upper_out)]):
             writes.append(pltpu.make_async_copy(src.at[part], dst.at[part], out_sem.at[i, part]))
@@ -419,7 +432,7 @@
                 pltpu.VMEM((2, width // 2, 2 * width), F32),
                 pltpu.VMEM((3, energies, width, depth), BF16),
                 pltpu.VMEM((3, long, 2 * width), BF16),
-                pltpu.VMEM((3, 2 * width, long), BF16),
+                pltpu.VMEM((3, width, 2 * width), F32),
                 pltpu.VMEM((2 * width, 2 * width), F32),
                 pltpu.VMEM((2, width, width), F32),
                 pltpu.VMEM((2, width, width), F32),

time: 29.7 us -> 28.5 us (0.960); the launches traced: 29.5 us -> 28 us
  Pallas kernels: 28.9 us -> 27.3 us
    pallas_call x1, Pallas kernels: 26.4 us -> 24.9 us  [per_device(): pl.pallas_call(functools.partial(kernel, energies, cells), out_shape=(sha...]
where the time goes in v5:
time: 28.5 us; the launch traced here: 28 us
  Pallas kernels  27.3 us (96%)
  between operations  0.64 us (2%)
    pallas_call x1, Pallas kernels, per_device(): pl.pallas_call(functools.partial(kernel, energies, cells), out_shape=(sha...  24.9 us
    pallas_call x1, Pallas kernels, per_device(): pl.pallas_call(deliver, out_shape=(shape, shape), in_specs=[pl.BlockSpec(...  2.47 us

profile of v5, /device:TPU:1, one launch (start us, length us, event | category | flops | bytes accessed | tf_op | source)
XLA Modules:
  0.0 28.0 jit_solution(4293057288055668204)
XLA Ops:
  0.6 24.9 %screen.1 = (f32[2,320,320]{2,1,0:T(8,128)}, f32[2,320,320]{2,1,0:T(8,128)}) custom-call(s32[4]{0:T(128)} %offsets.1, s32[8]{0:T(128)} %orbitals.1, f32[2,4,80,320]{3,2,1,0:T(8,128)} %bitcast.10, f32[2,4,80,320]{3,2,1,0:T(8,128)} %bitcast.11, f32[320,320]{1,0:T(8,128)} %bitcast.14, f32[320,320]{1,0:T(8,128)} %bitcast.15), custom_call_target="tpu_custom_call" | custom-call | flops 3145728000 | bytes 3276800 | tf_op jit(solution)/shard_map/screen/pallas_call | solution.py:417
  25.5 2.5 %deliver.1 = (f32[2,320,320]{2,1,0:T(8,128)}, f32[2,320,320]{2,1,0:T(8,128)}) custom-call(f32[2,320,320]{2,1,0:T(8,128)} %get-tuple-element.6.diag_in, f32[2,320,320]{2,1,0:T(8,128)} %get-tuple-element.7.upper_in), custom_call_target="tpu_custom_call" | custom-call | bytes 3276800 | tf_op jit(solution)/shard_map/deliver/pallas_call | solution.py:456

commit v6 on v3

--- a/solution.py
+++ b/solution.py
@@ -371,18 +371,25 @@
         write.wait()
 
 
-def deliver(diag_in, upper_in, diag, upper, sem):
+def deliver(diag_in, upper_in, diag, upper, held, in_sem, out_sem):
     rows = diag_in.shape[1]
     middle = rows // 16 * 8
     copies = []
     for i, (src, dst) in enumerate([(diag_in, diag), (upper_in, upper)]):
         for part in range(2):
             for j, at in enumerate([pl.ds(0, middle), pl.ds(middle, rows - middle)]):
-                copies.append(pltpu.make_async_copy(src.at[part, at], dst.at[part, at], sem.at[i, part, j]))
-    for copy in copies:
-        copy.start()
-    for copy in copies:
-        copy.wait()
+                here = held.at[i, part, at]
+                copies.append((
+                    pltpu.make_async_copy(src.at[part, at], here, in_sem.at[i, part, j]),
+                    pltpu.make_async_copy(here, dst.at[part, at], out_sem.at[i, part, j]),
+                ))
+    for arriving, _ in copies:
+        arriving.start()
+    for arriving, leaving in copies:
+        arriving.wait()
+        leaving.start()
+    for _, leaving in copies:
+        leaving.wait()
 
 
 def solution(mesh):
@@ -444,7 +451,7 @@
             out_shape=(shape, shape),
             in_specs=[pl.BlockSpec(memory_space=pl.ANY)] * 2,
             out_specs=(pl.BlockSpec(memory_space=pl.ANY),) * 2,
-            scratch_shapes=[dma((2, 2, 2))],
+            scratch_shapes=[pltpu.VMEM((2,) + shape.shape, F32), dma((2, 2, 2)), dma((2, 2, 2))],
             cost_estimate=pl.CostEstimate(
                 flops=0, bytes_accessed=16 * width * width * 2, transcendentals=0
             ),

time: 85.6 us -> 27.4 us (0.32)
  Pallas kernels: 84.8 us -> 26.5 us
    pallas_call x1, Pallas kernels: 60.7 us -> 2.47 us  [per_device(): pl.pallas_call(deliver, out_shape=(shape, shape), in_specs=[pl.BlockSpec(...]
where the time goes in v6:
time: 27.4 us; the launch traced here: 27.2 us
  Pallas kernels  26.5 us (97%)
  between operations  0.64 us (2%)
    pallas_call x1, Pallas kernels, per_device(): pl.pallas_call(functools.partial(kernel, energies, cells), out_shape=(sha...  24.1 us
    pallas_call x1, Pallas kernels, per_device(): pl.pallas_call(deliver, out_shape=(shape, shape), in_specs=[pl.BlockSpec(...  2.47 us

profile of v6, /device:TPU:1, one launch (start us, length us, event | category | flops | bytes accessed | tf_op | source)
XLA Modules:
  0.0 27.2 jit_solution(392783571274441674)
XLA Ops:
  0.6 24.1 %screen.1 = (f32[2,320,320]{2,1,0:T(8,128)}, f32[2,320,320]{2,1,0:T(8,128)}) custom-call(s32[4]{0:T(128)} %offsets.1, s32[8]{0:T(128)} %orbitals.1, f32[2,4,80,320]{3,2,1,0:T(8,128)} %bitcast.10, f32[2,4,80,320]{3,2,1,0:T(8,128)} %bitcast.11, f32[320,320]{1,0:T(8,128)} %bitcast.14, f32[320,320]{1,0:T(8,128)} %bitcast.15), custom_call_target="tpu_custom_call" | custom-call | flops 3145728000 | bytes 3276800 | tf_op jit(solution)/shard_map/screen/pallas_call | solution.py:410
  24.7 2.5 %deliver.1 = (f32[2,320,320]{2,1,0:T(8,128)}, f32[2,320,320]{2,1,0:T(8,128)}) custom-call(f32[2,320,320]{2,1,0:T(8,128)} %get-tuple-element.6.diag_in, f32[2,320,320]{2,1,0:T(8,128)} %get-tuple-element.7.upper_in), custom_call_target="tpu_custom_call" | custom-call | bytes 3276800 | tf_op jit(solution)/shard_map/deliver/pallas_call | solution.py:449
